TPU v7x, 256 devices: a whole 4x4x8 slice. The times are simulated.
256 devices in a mesh: ctx: 2 (over x_hi), tok: 16 (over z, core), head: 8 (over y, x_lo).
Axes of the slice: x: 4 (x_hi: 2, x_lo: 2; x = x_hi * 2 + x_lo), y: 4, z: 8, core: 2. Of those that a mesh axis runs over, the one named last changes fastest.
Arguments:
- keys: bfloat16 [2, 2, 16, 12288, 256], P(None, 'ctx', 'head', 'tok'), may hold values from -6 to 6
- values: bfloat16 [2, 2, 16, 12288, 256], P(None, 'ctx', 'head', 'tok'), may hold values from -6 to 6
- queries: bfloat16 [2, 2, 16, 12288, 256], P(None, 'ctx', 'head', 'tok'), may hold values from -6 to 6
- rates: float32 [2, 2, 16, 12288], P(None, 'ctx', 'head', 'tok'), may hold values from 0.1 to 3, as said below
- state_in: bfloat16 [2, 16, 3, 256, 512], P('ctx', 'head'), may hold values from -0.375 to 0.375
- fresh: bfloat16 [16, 3, 256, 512], P('head'), may hold values from -0.375 to 0.375
Outputs:
- outputs: bfloat16 [2, 2, 16, 12288, 256], P(None, 'ctx', 'head', 'tok')
Inputs may be any that keep to these rules, and one draw needn't show every extreme that they name: Positive per-token learning rates.
All inputs are finite; a program needn't handle non-finite values.
Results may differ from a plain program's by a relative error of at most 0.023.
Values may be sent and summed in bfloat16 or wider, within the bound.
A program may use at most 64 MiB of HBM per device.

v0:
```python
import jax
import jax.numpy as jnp
from jax import lax
from jax.sharding import Mesh
from jax.sharding import PartitionSpec as P

TOK = ("tok_0", "tok_1")


def filled_up(lines, size):
    spare = -len(lines) % size
    return jnp.pad(lines, [(0, spare)] + [(0, 0)] * (lines.ndim - 1))


def copy_for_each(value, axis):
    copies = jnp.broadcast_to(value, (lax.axis_size(axis), *value.shape))
    return lax.all_to_all(copies, axis, split_axis=0, concat_axis=0, tiled=True)


def laid_out(blocks, dim):
    blocks = jnp.moveaxis(blocks, 0, dim)
    shape = blocks.shape
    return blocks.reshape(*shape[:dim], shape[dim] * shape[dim + 1], *shape[dim + 2 :])


def gather_axes(value, axes, dim):
    far, near = axes
    first = copy_for_each(value, far)
    blocks = jnp.swapaxes(copy_for_each(first, near), 0, 1)
    return laid_out(blocks.reshape(-1, *value.shape), dim)


def cut_along(value, dim, size):
    shape = value.shape
    blocks = value.reshape(*shape[:dim], size, shape[dim] // size, *shape[dim + 1 :])
    return jnp.moveaxis(blocks, dim, 0)


def sum_at_owner(value, axis, dim):
    blocks = cut_along(value, dim, lax.axis_size(axis))
    arrived = lax.all_to_all(blocks, axis, split_axis=0, concat_axis=0, tiled=True)
    return arrived.astype(jnp.float32).sum(axis=0)


def sum_by_axis(value, axes, dim):
    far, near = axes
    own = sum_at_owner(cut_along(value, dim, lax.axis_size(far)), near, dim + 1)
    return jnp.sum(
        lax.all_to_all(own.astype(jnp.bfloat16), far, 0, 0, tiled=True).astype(jnp.float32), axis=0
    )


def sum_by_parts(value, axes):
    lines = value.reshape(-1, value.shape[-1])
    padded = filled_up(lines, lax.axis_size(axes[0]) * lax.axis_size(axes[1]))
    whole = gather_axes(sum_by_axis(padded, axes, 0).astype(jnp.bfloat16), axes, 0)
    return lax.slice_in_dim(whole, 0, len(lines)).reshape(value.shape).astype(jnp.float32)


def over_copies(value, axis):
    everything = copy_for_each(value, axis)
    return jnp.sum(everything, axis=0)


def from_behind(value, axis, steps):
    count = lax.axis_size(axis)
    first, last = (max(0, -steps), min(count, count - steps))
    return lax.ppermute(value, axis, [(source, source + steps) for source in range(first, last)])


def partial_grads(state, keys_p, values_p, rate_p):
    h_one = jnp.dot(keys_p, state[0], preferred_element_type=jnp.float32)
    h_three = jnp.dot(keys_p, state[1], preferred_element_type=jnp.float32)
    sig = jax.nn.sigmoid(h_one)
    act = (h_one * sig * h_three).astype(jnp.bfloat16)
    weighted = (rate_p[:, None] * values_p.astype(jnp.float32)).astype(jnp.bfloat16)
    dact = -jnp.dot(weighted, state[2], preferred_element_type=jnp.float32)
    d_one = (dact * h_three * sig * (1.0 + h_one * (1.0 - sig))).astype(jnp.bfloat16)
    d_three = (dact * h_one * sig).astype(jnp.bfloat16)
    contract = (((0,), (0,)), ((), ()))
    g_one = lax.dot_general(keys_p, d_one, contract, preferred_element_type=jnp.float32)
    g_three = lax.dot_general(keys_p, d_three, contract, preferred_element_type=jnp.float32)
    g_back = -lax.dot_general(weighted, act, contract, preferred_element_type=jnp.float32)
    return jnp.stack([g_one, g_three, g_back])


def apply_state(state, queries_h):
    p_one = jnp.dot(queries_h, state[0], preferred_element_type=jnp.float32)
    p_three = jnp.dot(queries_h, state[1], preferred_element_type=jnp.float32)
    mixed = (jax.nn.silu(p_one) * p_three).astype(jnp.bfloat16)
    contract = (((1,), (1,)), ((), ()))
    return lax.dot_general(mixed, state[2], contract, preferred_element_type=jnp.float32).astype(
        jnp.bfloat16
    )


def renormed(older_bf, grads, total_sq, heads_all, hidden):
    scale = 0.5 * jnp.sqrt(jnp.float32(3 * hidden * heads_all)) / jnp.sqrt(total_sq + 1e-06)
    older = older_bf.astype(jnp.float32)
    moved = older - scale * grads
    old_norm = jnp.sqrt(jnp.sum(older * older, axis=-2, keepdims=True))
    new_norm = jnp.sqrt(jnp.sum(moved * moved, axis=-2, keepdims=True) + 1e-06)
    return (moved * old_norm / new_norm).astype(jnp.bfloat16)


def block_tick(state, keys_t, values_t, rates_t, queries_t):
    heads_all = lax.axis_size("head") * state.shape[0]
    hidden = state.shape[3]
    grads = jax.vmap(partial_grads)(state, keys_t, values_t, rates_t)
    summed = sum_by_parts(grads.astype(jnp.bfloat16), ("tok_0", "tok_1"))
    total_sq = over_copies(jnp.sum(summed * summed), "head")
    newer = renormed(state, summed, total_sq, heads_all, hidden)
    applied = jax.vmap(apply_state)(newer, queries_t)
    return (newer, applied)


def shards(keys, values, queries, rates, state_in, fresh):
    first_state, first_out = block_tick(
        state_in[0], keys[0, 0], values[0, 0], rates[0, 0], queries[0, 0]
    )
    arrived = from_behind(first_state, "ctx", 1)
    incoming = jnp.where(lax.axis_index("ctx") == 0, fresh, arrived)
    second_state, second_out = block_tick(
        incoming, keys[1, 0], values[1, 0], rates[1, 0], queries[1, 0]
    )
    return jnp.stack([first_out, second_out])[:, None]


def solution(mesh):
    split = Mesh(
        mesh.devices.reshape(mesh.shape["ctx"], 8, 2, mesh.shape["head"]),
        ("ctx", "tok_0", "tok_1", "head"),
    )
    in_specs = (
        P(None, "ctx", "head", TOK, None),
        P(None, "ctx", "head", TOK, None),
        P(None, "ctx", "head", TOK, None),
        P(None, "ctx", "head", TOK),
        P("ctx", "head", None, None, None),
        P("head", None, None, None),
    )
    out_specs = P(None, "ctx", "head", TOK, None)
    return jax.shard_map(
        shards, mesh=split, in_specs=in_specs, out_specs=out_specs, check_vma=False
    )
```

profile of v0, /device:TPU:5, one launch (start us, length us, event | category | flops | bytes accessed | tf_op | source)
XLA Modules:
  0.0 229.8 jit_solution(878871744459939835)
XLA Ops:
  0.0 1.6 copy.176
  4.5 1.4 fusion.63
  5.9 1.5 fusion.52
  7.5 1.2 fusion.56
  9.2 5.3 %all_to_all.52 = bf16[2,8,96,512]{3,2,1,0:T(8,128)(2,1)S(1)} all-to-all(bf16[2,8,96,512]{3,2,1,0:T(8,128)(2,1)S(1)} %copy.108), channel_id=1, replica_groups=mesh['ctx'=2,'tok_0'=8,'tok_1'=2,'head'=8] {'tok_1'}, dimensions={0} | all-to-all | bytes 3145728 | tf_op jit(solution)/shard_map/all_to_all | solution.py:41
  15.2 30.3 %all_to_all.53 = bf16[8,96,512]{2,1,0:T(8,128)(2,1)S(1)} all-to-all(bf16[8,96,512]{2,1,0:T(8,128)(2,1)S(1)} %reduce_sum.120), channel_id=1, replica_groups=mesh['ctx'=2,'tok_0'=8,'tok_1'=2,'head'=8] {'tok_0'}, dimensions={0} | all-to-all | bytes 1572864 | tf_op jit(solution)/shard_map/all_to_all | solution.py:49
  45.7 22.9 %all_to_all.54 = bf16[8,96,512]{2,1,0:T(8,128)(2,1)S(1)} all-to-all(bf16[8,96,512]{2,1,0:T(8,128)(2,1)S(1)} %broadcast_in_dim.25), channel_id=1, replica_groups=mesh['ctx'=2,'tok_0'=8,'tok_1'=2,'head'=8] {'tok_0'}, dimensions={0} | all-to-all | bytes 1572864 | tf_op jit(solution)/shard_map/all_to_all | solution.py:17
  68.7 8.2 %all_to_all.55 = bf16[2,8,96,512]{3,2,1,0:T(8,128)(2,1)S(1)} all-to-all(bf16[2,8,96,512]{3,2,1,0:T(8,128)(2,1)S(1)} %broadcast_in_dim.26), channel_id=1, replica_groups=mesh['ctx'=2,'tok_0'=8,'tok_1'=2,'head'=8] {'tok_1'}, dimensions={0} | all-to-all | bytes 3145728 | tf_op jit(solution)/shard_map/all_to_all | solution.py:17
  77.0 1.4 fusion.1
  79.0 9.6 %all_to_all.56 = f32[8,1,1]{2,1,0:T(1,128)S(1)} all-to-all(f32[8,1,1]{2,1,0:T(1,128)S(1)} %broadcast_in_dim.27), channel_id=1, replica_groups=mesh['ctx'=2,'tok_0'=8,'tok_1'=2,'head'=8] {'head'}, dimensions={0} | all-to-all | bytes 64 | tf_op jit(solution)/shard_map/all_to_all | solution.py:17
  91.1 1.7 divide_convert_fusion.1
  92.8 1.6 collective-permute-start
  94.4 36.3 %collective-permute-done = bf16[2,3,256,512]{3,2,0,1:T(8,128)(2,1)} collective-permute-done((bf16[2,3,256,512]{3,2,0,1:T(8,128)(2,1)}, bf16[2,3,256,512]{3,2,0,1:T(8,128)(2,1)}, u32[]{:S(2)}, u32[]{:S(2)}) %collective-permute-start) | collective-permute-done | bytes 1572896 | tf_op jit(solution)/shard_map/ppermute | solution.py:68
  130.7 2.0 copy_select_fusion
  133.9 0.8 copy-done.5
  135.4 1.4 fusion.60
  136.8 1.5 fusion.53
  138.4 1.2 fusion.57
  140.1 7.4 %all_to_all.57 = bf16[2,8,96,512]{3,2,1,0:T(8,128)(2,1)S(1)} all-to-all(bf16[2,8,96,512]{3,2,1,0:T(8,128)(2,1)S(1)} %copy.125), channel_id=1, replica_groups=mesh['ctx'=2,'tok_0'=8,'tok_1'=2,'head'=8] {'tok_1'}, dimensions={0} | all-to-all | bytes 3145728 | tf_op jit(solution)/shard_map/all_to_all | solution.py:41
  147.5 1.4 reduce_sum.126
  148.8 27.0 %all_to_all.58 = bf16[8,96,512]{2,1,0:T(8,128)(2,1)S(1)} all-to-all(bf16[8,96,512]{2,1,0:T(8,128)(2,1)} %reduce_sum.126), channel_id=1, replica_groups=mesh['ctx'=2,'tok_0'=8,'tok_1'=2,'head'=8] {'tok_0'}, dimensions={0} | all-to-all | bytes 1572864 | tf_op jit(solution)/shard_map/all_to_all | solution.py:49
  176.0 0.9 broadcast_in_dim.28
  176.9 3.5 %all-to-all-start.7 = ((bf16[8,96,512]{2,1,0:T(8,128)(2,1)}), bf16[8,96,512]{2,1,0:T(8,128)(2,1)S(1)}, u32[]{:S(2)}, u32[]{:S(2)}) async-start(bf16[8,96,512]{2,1,0:T(8,128)(2,1)} %broadcast_in_dim.28), calls=%async_computation.7 | async-start | bytes 1572864 | tf_op jit(solution)/shard_map/all_to_all | solution.py:17
  180.5 3.5 %fusion.74 = f32[2,512,768]{1,2,0:T(8,128)} fusion(bf16[2,1,2,768,256]{4,3,2,1,0:T(8,128)(2,1)} %param.8, bf16[2,3,256,512]{3,2,0,1:T(8,128)(2,1)} %divide_convert_fusion.1), kind=kOutput, calls=%fused_computation.92 | convolution fusion | flops 402653184 | bytes 4456448 | tf_op jit(solution)/shard_map/vmap()/dot_general | solution.py:88
  184.0 4.6 %fusion.46 = bf16[1,2,768,256]{3,2,1,0:T(8,128)(2,1)} fusion(f32[2,512,768]{1,2,0:T(8,128)} %fusion.74, bf16[2,1,2,768,256]{4,3,2,1,0:T(8,128)(2,1)} %param.8, bf16[2,3,256,512]{3,2,0,1:T(8,128)(2,1)} %divide_convert_fusion.1), kind=kOutput, calls=%fused_computation.73 | convolution fusion | flops 810418176 | bytes 5767168 | tf_op jit(solution)/shard_map/vmap()/dot_general | solution.py:92
  188.6 15.5 %all-to-all-done.7 = bf16[8,96,512]{2,1,0:T(8,128)(2,1)S(1)} async-done(((bf16[8,96,512]{2,1,0:T(8,128)(2,1)}), bf16[8,96,512]{2,1,0:T(8,128)(2,1)S(1)}, u32[]{:S(2)}, u32[]{:S(2)}) %all-to-all-start.7) | async-done | bytes 786464 | tf_op jit(solution)/shard_map/all_to_all | solution.py:17
  204.2 5.1 %all_to_all.59 = bf16[2,8,96,512]{3,2,1,0:T(8,128)(2,1)S(1)} all-to-all(bf16[2,8,96,512]{3,2,1,0:T(8,128)(2,1)S(1)} %broadcast_in_dim.29), channel_id=1, replica_groups=mesh['ctx'=2,'tok_0'=8,'tok_1'=2,'head'=8] {'tok_1'}, dimensions={0} | all-to-all | bytes 3145728 | tf_op jit(solution)/shard_map/all_to_all | solution.py:17
  209.3 1.4 fusion.3
  211.4 7.4 %all_to_all.60 = f32[8,1,1]{2,1,0:T(1,128)S(1)} all-to-all(f32[8,1,1]{2,1,0:T(1,128)S(1)} %broadcast_in_dim.30), channel_id=1, replica_groups=mesh['ctx'=2,'tok_0'=8,'tok_1'=2,'head'=8] {'head'}, dimensions={0} | all-to-all | bytes 64 | tf_op jit(solution)/shard_map/all_to_all | solution.py:17
  221.8 1.1 copy-done.3
  223.5 3.6 %fusion.47 = bf16[1,2,768,256]{3,2,1,0:T(8,128)(2,1)} fusion(f32[2,512,768]{1,2,0:T(8,128)S(1)} %fusion.64, bf16[2,1,2,768,256]{4,3,2,1,0:T(8,128)(2,1)} %param.8, bf16[2,3,256,512]{3,2,0,1:T(8,128)(2,1)} %copy-done.3), kind=kOutput, calls=%fused_computation.74 | convolution fusion | flops 810418176 | bytes 5767168 | tf_op jit(solution)/shard_map/vmap()/dot_general | solution.py:92
  227.1 2.7 %maximum_bitcast_fusion.2 = bf16[2,1,2,768,256]{4,3,2,1,0:T(8,128)(2,1)} fusion(bf16[1,2,768,256]{3,2,1,0:T(8,128)(2,1)} %fusion.47, bf16[1,2,768,256]{3,2,1,0:T(8,128)(2,1)} %fusion.46), kind=kLoop, calls=%fused_computation.52 | loop fusion | flops 786432 | bytes 3145728 | tf_op jit(solution)/shard_map/broadcast_in_dim | solution.py:126
  (47 shorter events, 12.8 us)
Async XLA Ops:
  0.0 1.9 copy-start.1
  2.5 0.7 copy-start.7
  2.5 1.4 copy-start.4
  76.9 13.4 %copy-start = (bf16[1,2,3,256,512]{4,3,2,1,0:T(8,128)(2,1)S(1)}, bf16[1,2,3,256,512]{4,3,2,1,0:T(8,128)(2,1)}, u32[]{:S(2)}) copy-start(bf16[1,2,3,256,512]{4,3,2,1,0:T(8,128)(2,1)} %param.10) | copy-start | bytes 4718596
  92.8 40.0 %copy-start.2 = (bf16[2,1,2,768,256]{4,3,2,1,0:T(8,128)(2,1)S(1)}, bf16[2,1,2,768,256]{4,3,2,1,0:T(8,128)(2,1)}, u32[]{:S(2)}) copy-start(bf16[2,1,2,768,256]{4,3,2,1,0:T(8,128)(2,1)} %param.6) | copy-start | bytes 4718596
  92.8 37.9 %collective-permute-start = (bf16[2,3,256,512]{3,2,0,1:T(8,128)(2,1)}, bf16[2,3,256,512]{3,2,0,1:T(8,128)(2,1)}, u32[]{:S(2)}, u32[]{:S(2)}) collective-permute-start(bf16[2,3,256,512]{3,2,0,1:T(8,128)(2,1)} %divide_convert_fusion.1), channel_id=1, source_target_pairs={{0,128},{1,129},{2,130},{3,131},{4,132},{5,133},{6,134},{7,135},{8... | collective-permute-start | bytes 4718600 | tf_op jit(solution)/shard_map/ppermute | solution.py:68
  133.4 1.4 copy-start.5
  176.9 27.1 %all-to-all-start.7 = ((bf16[8,96,512]{2,1,0:T(8,128)(2,1)}), bf16[8,96,512]{2,1,0:T(8,128)(2,1)S(1)}, u32[]{:S(2)}, u32[]{:S(2)}) async-start(bf16[8,96,512]{2,1,0:T(8,128)(2,1)} %broadcast_in_dim.28), calls=%async_computation.7 | async-start | bytes 1572864 | tf_op jit(solution)/shard_map/all_to_all | solution.py:17
  221.2 1.7 copy-start.6
  221.8 1.1 copy-start.3
where the time goes:
time: 231 us; the launch traced here: 230 us
  blocking collectives  123 us (53%)
  waiting for transfers between devices  51.8 us (22%)
  matrix products  24.1 us (10%)
  other arithmetic  15.9 us (7%)
  local copies, waits for them, and re-layouts  7.96 us (3%)
  starting transfers between devices  5.14 us (2%)
    all_to_all x2, blocking collectives, sum_by_axis(): lax.all_to_all(own.astype(jnp.bfloat16), far, 0, 0, tiled=True)  57.3 us
    all_to_all x5, blocking collectives, copy_for_each(): return lax.all_to_all(copies, axis, split_axis=0, concat_axis=0, tiled=True)  53.2 us
    ppermute x1, waiting for transfers between devices, from_behind(): lax.ppermute(value, axis, [(source, source + steps) for source in range(f...  36.3 us
    all_to_all x1, waiting for transfers between devices, copy_for_each(): return lax.all_to_all(copies, axis, split_axis=0, concat_axis=0, tiled=True)  15.5 us
    all_to_all x2, blocking collectives, sum_at_owner(): lax.all_to_all(blocks, axis, split_axis=0, concat_axis=0, tiled=True)  12.7 us
    dot_general x2, matrix products, apply_state(): lax.dot_general(mixed, state[2], contract, preferred_element_type=jnp.flo...  8.19 us
    unnamed x17, local copies, waits for them, and re-layouts  4.7 us
  transfers between devices with their start and end apart: 2, of which 2 were waited for; matrix products, arithmetic and copies ran while one was open for 4% of the time, Pallas kernels for 0%

commit v1 on v0

v1 whole, which is shorter than its diff:
```python
import functools

import jax
import jax.numpy as jnp
from jax import lax
from jax.experimental import pallas as pl
from jax.experimental.pallas import tpu as pltpu
from jax.sharding import PartitionSpec as P

MESH = pl.DeviceIdType.MESH
F32, BF16 = jnp.float32, jnp.bfloat16
NT = (((1,), (1,)), ((), ()))


def sigmoid(x):
    return 0.5 * jnp.tanh(0.5 * x) + 0.5


def kernel(
    sizes,
    keys, values, queries, rates, state_in, fresh,
    out,
    k0, v0, k1, v1, qs, os_, rt, rtp, s0, so, s1, s2, s3,
    kt0, rv0, rvt0, kt1, rv1, rvt1, act, d1, d3,
    gx, gxr, gb, gg, rin, rhalf, rout,
    sqp, sqs, sqz, sqo,
    load_sem, osem, xs, xr, gxs, gxrs, rs_s, rs_r, ag_s, ag_r, ho_s, ho_r, st_s, st_r,
    pp_s, pp_r, zz_s, zz_r, zo_s, zo_r, os_s, os_r,
):
    nz, nh, tok, dh, df, heads_all = sizes
    rows = dh // nz
    half = rows // 2
    c, t, h = lax.axis_index("ctx"), lax.axis_index("tok"), lax.axis_index("head")
    z, core = t // 2, t % 2
    other = 1 - core
    np_ = 2 * nh
    me_p = h * 2 + core

    def zdev(step):
        return (c, lax.rem(z + step + nz, nz) * 2 + core, h)

    def pdev(j):
        p = lax.rem(me_p + j, np_)
        return (c, z * 2 + lax.rem(p, 2), p // 2)

    def odev(step):
        return (1 - c, lax.rem(z + step, nz) * 2 + core, h)

    mate = (c, z * 2 + other, h)
    twin = (1 - c, t, h)

    local = [
        (keys.at[0, 0, other], k0.at[1]),
        (state_in.at[0, other], s0.at[1]),
        (values.at[0, 0, other], v0.at[1]),
        (rates, rt),
        (keys.at[0, 0, core], k0.at[0]),
        (state_in.at[0, core], s0.at[0]),
        (values.at[0, 0, core], v0.at[0]),
        (keys.at[1, 0, core], k1.at[0]),
        (values.at[1, 0, core], v1.at[0]),
        (queries.at[0, 0, core], qs.at[0, 0]),
        (queries.at[1, 0, core], qs.at[1, 0]),
    ]
    loads = [pltpu.make_async_copy(a, b, load_sem.at[i]) for i, (a, b) in enumerate(local)]
    for cp in loads:
        cp.start()
    fresh_load = pltpu.make_async_copy(fresh.at[core], s2, load_sem.at[len(local)])

    @pl.when(c == 0)
    def _():
        fresh_load.start()

    barrier = pltpu.get_barrier_semaphore()
    for j in range(1, np_):
        pl.semaphore_signal(barrier, inc=1, device_id=pdev(j), device_id_type=MESH)
    for j in range(1, nz):
        pl.semaphore_signal(barrier, inc=1, device_id=zdev(j), device_id_type=MESH)
    for j in range(nz):
        pl.semaphore_signal(barrier, inc=1, device_id=odev(j), device_id_type=MESH)

    def remote(src, dst, ss, rs, dev):
        return pltpu.make_async_remote_copy(
            src_ref=src, dst_ref=dst, send_sem=ss, recv_sem=rs, device_id=dev, device_id_type=MESH
        )

    def rate_columns(ref, tick, head):
        row = jnp.where(head == 0, ref[tick, 0, 0:1, :], ref[tick, 0, 1:2, :])
        col = jnp.broadcast_to(row, (128, tok)).T
        return jnp.concatenate([col] * (dh // 128), axis=1)

    def prepare(k, v, col, kt, rv, rvt, lo):
        kt[:, lo:lo + tok] = k[...].T
        weighted = (v[...].astype(F32) * col).astype(BF16)
        rv[lo:lo + tok, :] = weighted
        rvt[:, lo:lo + tok] = weighted.T

    def forward(k, rv, state, lo):
        tile = 256
        for i in range(tok // tile):
            a = lo + i * tile
            kk = k[i * tile:(i + 1) * tile, :]
            h1 = jnp.dot(kk, state[0], preferred_element_type=F32)
            h3 = jnp.dot(kk, state[1], preferred_element_type=F32)
            dact = jnp.dot(rv[a:a + tile, :], state[2], preferred_element_type=F32)
            sig = sigmoid(h1)
            hs = h1 * sig
            act[a:a + tile, :] = (hs * h3).astype(BF16)
            d3[a:a + tile, :] = (dact * hs).astype(BF16)
            d1[a:a + tile, :] = (dact * h3 * (sig + hs * (1.0 - sig))).astype(BF16)

    def grad(m, kt, rvt, lo, hi):
        left, right = ((kt, d1), (kt, d3), (rvt, act))[m]
        return jnp.dot(left[:, lo:hi], right[lo:hi, :], preferred_element_type=F32)

    order = (2, 0, 1)

    for i in (0, 1, 2, 3):
        loads[i].wait()
    prepare(k0.at[1], v0.at[1], rate_columns(rt, 0, other), kt0, rv0, rvt0, 0)
    forward(k0.at[1], rv0, s0.at[1], 0)
    for m in order:
        gx[m] = grad(m, kt0, rvt0, 0, tok).astype(BF16)

    pl.semaphore_wait(barrier, np_ - 1 + nz - 1 + nz)

    gx_copies = {m: remote(gx.at[m], gxr.at[m], gxs.at[m], gxrs.at[m], mate) for m in order}
    for m in order:
        gx_copies[m].start()
    state_copy = remote(s0.at[0], so, st_s, st_r, twin)
    for i in (4, 5, 6):
        loads[i].wait()

    @pl.when(c == 0)
    def _():
        state_copy.start()

    mate_copies = [
        remote(src, dst, xs.at[i], xr.at[i], mate)
        for i, (src, dst) in enumerate([
            (rates, rtp),
            (keys.at[1, 0, other], k1.at[1]),
            (values.at[1, 0, other], v1.at[1]),
            (queries.at[0, 0, other], qs.at[0, 1]),
            (queries.at[1, 0, other], qs.at[1, 1]),
        ])
    ]
    for cp in mate_copies:
        cp.start()

    prepare(k0.at[0], v0.at[0], rate_columns(rt, 0, core), kt0, rv0, rvt0, tok)
    forward(k0.at[0], rv0, s0.at[0], tok)

    def chunk(owner_step, m, part=None):
        owner = lax.rem(z + owner_step + 2 * nz, nz)
        if part is None:
            return (m, pl.ds(pl.multiple_of(owner * rows, rows), rows), slice(None))
        return (m, pl.ds(pl.multiple_of(owner * rows + part * half, half), half), slice(None))

    sides = ((0, -1), (1, 1))

    def rs_copy(tick, hop, d, s, m):
        if hop == 0:
            src, dst, dev = gb.at[(tick,) + chunk(3 * s, m)], rin.at[tick, 0, d, m], zdev(s)
        elif hop == 1:
            src, dst, dev = gb.at[(tick,) + chunk(4, m, d)], rhalf.at[tick, d, m], zdev(2 * s)
        else:
            src, dst, dev = rout.at[tick, hop - 2, d, m], rin.at[tick, hop - 1, d, m], zdev(s)
        return remote(src, dst, rs_s.at[tick, hop, d, m], rs_r.at[tick, hop, d, m], dev)

    def rs_first(tick, m):
        for d, s in sides:
            rs_copy(tick, 1, d, s, m).start()
            rs_copy(tick, 0, d, s, m).start()

    def rs_second(tick, m):
        for d, s in sides:
            rs_copy(tick, 0, d, s, m).wait_recv()
            rs_copy(tick, 1, d, s, m).wait_recv()
            own = gb[(tick,) + chunk(2 * s, m)].astype(F32) + rin[tick, 0, d, m].astype(F32)
            far = rhalf[tick, d, m].astype(F32)
            if d == 0:
                rout[tick, 0, d, m, 0:half, :] = (own[0:half] + far).astype(BF16)
                rout[tick, 0, d, m, half:rows, :] = own[half:rows].astype(BF16)
            else:
                rout[tick, 0, d, m, 0:half, :] = own[0:half].astype(BF16)
                rout[tick, 0, d, m, half:rows, :] = (own[half:rows] + far).astype(BF16)
            rs_copy(tick, 2, d, s, m).start()

    def rs_third(tick, m):
        for d, s in sides:
            rs_copy(tick, 2, d, s, m).wait_recv()
            own = gb[(tick,) + chunk(s, m)].astype(F32) + rin[tick, 1, d, m].astype(F32)
            rout[tick, 1, d, m] = own.astype(BF16)
            rs_copy(tick, 3, d, s, m).start()

    def rs_last(tick, m, buf):
        total = gb[(tick,) + chunk(0, m)].astype(F32)
        for d, s in sides:
            rs_copy(tick, 3, d, s, m).wait_recv()
            total = total + rin[tick, 2, d, m].astype(F32)
        gg[(buf,) + chunk(0, m)] = total.astype(BF16)
        square = total * total
        tile = jnp.zeros((8, 128), F32)
        for i in range(0, rows, 8):
            for j in range(0, df, 128):
                tile = tile + square[i:i + 8, j:j + 128]
        return tile

    def ag_copy(buf, hop, d, s, m):
        if hop == 0:
            part, dev = chunk(0, m), zdev(s)
        elif hop == 1:
            part, dev = chunk(-s, m), zdev(s)
        elif hop == 2:
            part, dev = chunk(-2 * s, m), zdev(s)
        else:
            part, dev = chunk(-2 * s, m, d), zdev(2 * s)
        part = (buf,) + part
        return remote(gg.at[part], gg.at[part], ag_s.at[buf, hop, d, m], ag_r.at[buf, hop, d, m], dev)

    def ag_first(buf, m):
        for d, s in sides:
            ag_copy(buf, 0, d, s, m).start()

    def ag_second(buf, m):
        for d, s in sides:
            ag_copy(buf, 0, d, s, m).wait_recv()
            ag_copy(buf, 1, d, s, m).start()

    def ag_third(buf, m):
        for d, s in sides:
            ag_copy(buf, 1, d, s, m).wait_recv()
            ag_copy(buf, 3, d, s, m).start()
            ag_copy(buf, 2, d, s, m).start()

    def ag_last(buf, m):
        for d, s in sides:
            ag_copy(buf, 3, d, s, m).wait_recv()
            ag_copy(buf, 2, d, s, m).wait_recv()

    def plane_copy(tick, j):
        return remote(sqp.at[tick, me_p], sqp.at[tick, me_p], pp_s.at[tick, j], pp_r.at[tick, j], pdev(j))

    def norm_first(tick, tile):
        sqp[tick, me_p] = tile
        for j in range(1, np_):
            plane_copy(tick, j).start()

    def z_copy(tick, j):
        return remote(sqs.at[tick], sqz.at[tick, z], zz_s.at[tick, j], zz_r.at[tick, j], zdev(j))

    def zo_copy(j):
        return remote(sqs.at[0], sqo.at[z], zo_s.at[j], zo_r.at[j], odev(j))

    def norm_second(tick):
        for j in range(1, np_):
            plane_copy(tick, j).wait_recv()
        total = sqp[tick, 0]
        for j in range(1, np_):
            total = total + sqp[tick, j]
        sqs[tick] = total
        sqz[tick, z] = total
        for j in range(1, nz):
            z_copy(tick, j).start()
        if tick == 0:
            @pl.when(c == 0)
            def _():
                for j in range(nz):
                    zo_copy(j).start()

    def scale_of(ref):
        total = ref[0]
        for j in range(1, nz):
            total = total + ref[j]
        sq = jnp.sum(jnp.sum(total, axis=1, keepdims=True), axis=0, keepdims=True)
        return 0.5 * jnp.sqrt(jnp.float32(3 * df * heads_all)) / jnp.sqrt(sq + 1e-06)

    def renorm(old, buf, scale, new, m):
        for j in range(0, df, 128):
            older = old[m, :, j:j + 128].astype(F32)
            moved = older + scale * gg[buf, m, :, j:j + 128].astype(F32)
            was = jnp.sum(older * older, axis=0, keepdims=True)
            now = jnp.sum(moved * moved, axis=0, keepdims=True)
            factor = jnp.sqrt(was) / jnp.sqrt(now + 1e-06)
            new[m, :, j:j + 128] = (moved * factor).astype(BF16)

    def apply(tick, part, state):
        tile = 256
        for i in range(tok // tile):
            at = slice(i * tile, (i + 1) * tile)
            q = qs[tick, part, at, :]
            p1 = jnp.dot(q, state[0], preferred_element_type=F32)
            p3 = jnp.dot(q, state[1], preferred_element_type=F32)
            pa = (p1 * sigmoid(p1) * p3).astype(BF16)
            os_[tick, part, at, :] = lax.dot_general(pa, state[2], NT, preferred_element_type=F32).astype(BF16)

    def own_out(tick):
        return pltpu.make_async_copy(os_.at[tick, 0], out.at[tick, 0, core], osem.at[tick])

    def mate_out(tick):
        return remote(os_.at[tick, 1], out.at[tick, 0, core], os_s.at[tick], os_r.at[tick], mate)

    for m in order:
        part = grad(m, kt0, rvt0, tok, 2 * tok).astype(BF16).astype(F32)
        gx_copies[m].wait_recv()
        gb[0, m] = (part + gxr[m].astype(F32)).astype(BF16)
        rs_first(0, m)
    loads[7].wait()
    loads[8].wait()
    prepare(k1.at[0], v1.at[0], rate_columns(rt, 1, core), kt1, rv1, rvt1, 0)
    for m in order:
        rs_second(0, m)
    for i in (0, 1, 2):
        mate_copies[i].wait_recv()
    prepare(k1.at[1], v1.at[1], rate_columns(rtp, 1, core), kt1, rv1, rvt1, tok)
    for m in order:
        rs_third(0, m)

    def hand_over(m):
        part = chunk(0, m)
        return remote(gg.at[(0,) + part], gg.at[(1,) + part], ho_s.at[m], ho_r.at[m], twin)

    tile = jnp.zeros((8, 128), F32)
    for m in order:
        tile = tile + rs_last(0, m, 0)

        @pl.when(c == 0)
        def _():
            hand_over(m).start()

        ag_first(0, m)
    norm_first(0, tile)

    @pl.when(c == 1)
    def _():
        for m in order:
            hand_over(m).wait_recv()
            ag_first(1, m)

    norm_second(0)

    @pl.when(c == 1)
    def _():
        for m in order:
            ag_second(1, m)
        for m in order:
            ag_third(1, m)
    for m in order:
        ag_second(0, m)

    @pl.when(c == 1)
    def _():
        for j in range(nz):
            zo_copy(j).wait_recv()
        state_copy.wait_recv()
        scale = scale_of(sqo)
        for m in order:
            ag_last(1, m)
            renorm(so, 1, scale, s2, m)

    @pl.when(c == 0)
    def _():
        fresh_load.wait()

    forward(k1.at[0], rv1, s2, 0)
    for m in order:
        ag_third(0, m)
    forward(k1.at[1], rv1, s2, tok)
    for m in order:
        gb[1, m] = grad(m, kt1, rvt1, 0, 2 * tok).astype(BF16)
        rs_first(1, m)
    for j in range(1, nz):
        z_copy(0, j).wait_recv()
    scale = scale_of(sqz.at[0])
    for m in order:
        ag_last(0, m)
        renorm(s0.at[0], 0, scale, s1, m)
    for m in order:
        rs_second(1, m)
    loads[9].wait()
    mate_copies[3].wait_recv()
    apply(0, 1, s1)
    mate_out(0).start()
    for m in order:
        rs_third(1, m)
    apply(0, 0, s1)
    own_out(0).start()
    tile = jnp.zeros((8, 128), F32)
    for m in order:
        tile = tile + rs_last(1, m, 2)
        ag_first(2, m)
    norm_first(1, tile)
    for m in order:
        ag_second(2, m)
    norm_second(1)
    for m in order:
        ag_third(2, m)
    loads[10].wait()
    mate_copies[4].wait_recv()
    for j in range(1, nz):
        z_copy(1, j).wait_recv()
    scale = scale_of(sqz.at[1])
    for m in order:
        ag_last(2, m)
        renorm(s2, 2, scale, s3, m)
    apply(1, 1, s3)
    mate_out(1).start()
    apply(1, 0, s3)
    own_out(1).start()

    for m in order:
        gx_copies[m].wait_send()
        for tick in (0, 1):
            for hop in range(4):
                for d, s in sides:
                    rs_copy(tick, hop, d, s, m).wait_send()
        for buf in (0, 2):
            for hop in range(4):
                for d, s in sides:
                    ag_copy(buf, hop, d, s, m).wait_send()
    for cp in mate_copies:
        cp.wait_send()
    for tick in (0, 1):
        for j in range(1, np_):
            plane_copy(tick, j).wait_send()
        for j in range(1, nz):
            z_copy(tick, j).wait_send()

    @pl.when(c == 0)
    def _():
        state_copy.wait_send()
        for m in order:
            hand_over(m).wait_send()
        for j in range(nz):
            zo_copy(j).wait_send()

    @pl.when(c == 1)
    def _():
        for m in order:
            for hop in range(4):
                for d, s in sides:
                    ag_copy(1, hop, d, s, m).wait_send()

    for tick in (0, 1):
        own_out(tick).wait()
        mate_out(tick).wait()


def shards(mesh_shape, keys, values, queries, rates, state_in, fresh):
    nz, nh = mesh_shape["tok"] // 2, mesh_shape["head"]
    _, _, _, tok, dh = keys.shape
    df = state_in.shape[-1]
    heads_all = 2 * nh
    rows = dh // nz
    sizes = (nz, nh, tok, dh, df, heads_all)
    dma = pltpu.SemaphoreType.DMA

    def vm(*shape, dtype=BF16):
        return pltpu.VMEM(shape, dtype)

    both = 2 * tok
    state = (3, dh, df)
    scratch = [
        vm(2, tok, dh), vm(2, tok, dh), vm(2, tok, dh), vm(2, tok, dh), vm(2, 2, tok, dh), vm(2, 2, tok, dh),
        vm(*rates.shape, dtype=F32), vm(*rates.shape, dtype=F32),
        vm(2, *state), vm(*state), vm(*state), vm(*state), vm(*state),
        vm(dh, both), vm(both, dh), vm(dh, both), vm(dh, both), vm(both, dh), vm(dh, both),
        vm(both, df), vm(both, df), vm(both, df),
        vm(*state), vm(*state), vm(2, *state), vm(3, *state),
        vm(2, 3, 2, 3, rows, df), vm(2, 2, 3, rows // 2, df), vm(2, 2, 2, 3, rows, df),
        vm(2, 2 * nh, 8, 128, dtype=F32), vm(2, 8, 128, dtype=F32), vm(2, nz, 8, 128, dtype=F32), vm(nz, 8, 128, dtype=F32),
        dma((12,)), dma((2,)), dma((5,)), dma((5,)), dma((3,)), dma((3,)),
        dma((2, 4, 2, 3)), dma((2, 4, 2, 3)), dma((3, 4, 2, 3)), dma((3, 4, 2, 3)),
        dma((3,)), dma((3,)), dma, dma,
        dma((2, 2 * nh)), dma((2, 2 * nh)), dma((2, nz)), dma((2, nz)), dma((nz,)), dma((nz,)),
        dma((2,)), dma((2,)),
    ]
    return pl.pallas_call(
        functools.partial(kernel, sizes),
        out_shape=jax.ShapeDtypeStruct(queries.shape, BF16),
        in_specs=[pl.BlockSpec(memory_space=pl.ANY)] * 6,
        out_specs=pl.BlockSpec(memory_space=pl.ANY),
        scratch_shapes=scratch,
        compiler_params=pltpu.CompilerParams(
            collective_id=0, has_side_effects=True, vmem_limit_bytes=56 * 1024 * 1024
        ),
        cost_estimate=pl.CostEstimate(flops=8_000_000_000, bytes_accessed=10_000_000, transcendentals=3_000_000),
    )(keys, values, queries, rates, state_in, fresh)


def solution(mesh):
    in_specs = (
        P(None, "ctx", "head", "tok", None),
        P(None, "ctx", "head", "tok", None),
        P(None, "ctx", "head", "tok", None),
        P(None, "ctx", "head", "tok"),
        P("ctx", "head", None, None, None),
        P("head", None, None, None),
    )
    return jax.shard_map(
        functools.partial(shards, dict(mesh.shape)),
        mesh=mesh,
        in_specs=in_specs,
        out_specs=P(None, "ctx", "head", "tok", None),
        check_vma=False,
    )
```

time: 231 us -> 82 us (0.35)
  blocking collectives: 123 us -> 0 us
  Pallas kernels: 0 us -> 79.3 us
  waiting for transfers between devices: 51.8 us -> 0 us
  matrix products: 24.1 us -> 0 us
  other arithmetic: 15.9 us -> 0 us
  local copies, waits for them, and re-layouts: 7.96 us -> 2.65 us
  starting transfers between devices: 5.14 us -> 0 us
    all_to_all x9 -> x0, blocking collectives: 123 us -> none  [the longest x2 57.3 us: sum_by_axis(): lax.all_to_all(own.astype(jnp.bfloat16), far, 0, 0, tiled=True)]
    pallas_call x0 -> x1, Pallas kernels: none -> 79.3 us  [shards(): pl.pallas_call(functools.partial(kernel, sizes), out_shape=jax.ShapeDtype...]
    ppermute x1 -> x0, waiting for transfers between devices: 36.3 us -> none  [from_behind(): lax.ppermute(value, axis, [(source, source + steps) for source in range(f...]
    dot_general x16 -> x0, matrix products: 24.1 us -> none  [the longest x2 8.19 us: apply_state(): lax.dot_general(mixed, state[2], contract, preferred_element_type=jnp.flo...]
    all_to_all x1 -> x0, waiting for transfers between devices: 15.5 us -> none  [copy_for_each(): return lax.all_to_all(copies, axis, split_axis=0, concat_axis=0, tiled=True)]
    reduce_sum x10 -> x0, other arithmetic: 7.68 us -> none  [the longest x2 2.81 us: block_tick(): total_sq = over_copies(jnp.sum(summed * summed), 'head')]
    all_to_all x1 -> x0, starting transfers between devices: 3.55 us -> none  [copy_for_each(): return lax.all_to_all(copies, axis, split_axis=0, concat_axis=0, tiled=True)]
    broadcast_in_dim x1 -> x0, other arithmetic: 2.66 us -> none  [shards(): return jnp.stack([first_out, second_out])[:, None]]
  transfers between devices with their start and end apart: 2 -> 0, of which waited for: 2 -> 0; matrix products, arithmetic and copies ran while one was open for 4% -> 0% of each run, Pallas kernels for 0% -> 0%
where the time goes in v1:
time: 82 us; the launch traced here: 81.9 us
  Pallas kernels  79.3 us (97%)
  local copies, waits for them, and re-layouts  2.65 us (3%)
    pallas_call x1, Pallas kernels, shards(): pl.pallas_call(functools.partial(kernel, sizes), out_shape=jax.ShapeDtype...  79.3 us
    unnamed x1, local copies, waits for them, and re-layouts  2.65 us

profile of v1, /device:TPU:5, one launch (start us, length us, event | category | flops | bytes accessed | tf_op | source)
XLA Modules:
  0.0 81.9 jit_solution(9333613084639511813)
XLA Ops:
  0.0 79.3 %shard_map.64 = bf16[2,1,2,768,256]{4,3,2,1,0:T(8,128)(2,1)} custom-call(bf16[2,1,2,768,256]{4,3,2,1,0:T(8,128)(2,1)} %keys.1, bf16[2,1,2,768,256]{4,3,2,1,0:T(8,128)(2,1)} %values.1, bf16[2,1,2,768,256]{4,3,2,1,0:T(8,128)(2,1)} %queries.1, f32[2,1,2,768]{3,2,1,0:T(2,128)} %rates.1, bf16[1,2,3,256,512]{4,3,2,1,0:T(8,128)(2,1)} %state_in.1, ...), custom_call_target="tpu_custom_call" | custom-call | flops 8000000000 | bytes 10000000 | tf_op jit(solution)/shard_map/pallas_call | solution.py:479
  79.3 2.7 %copy.8 = bf16[2,1,2,768,256]{4,3,2,1,0:T(8,128)(2,1)} copy(bf16[2,1,2,768,256]{4,3,2,1,0:T(8,128)(2,1)} %shard_map.64) | data formatting | bytes 3145728

commit v2 on v1

v2 whole, which is shorter than its diff:
```python
import functools

import jax
import jax.numpy as jnp
from jax import lax
from jax.experimental import pallas as pl
from jax.experimental.pallas import tpu as pltpu
from jax.sharding import PartitionSpec as P

MESH = pl.DeviceIdType.MESH
F32, BF16 = jnp.float32, jnp.bfloat16
LANES, GROUP = 128, 256
NT = (((1,), (1,)), ((), ()))


def sigmoid(x):
    return 0.5 * jnp.tanh(0.5 * x) + 0.5


def kernel(
    sizes,
    keys, values, queries, rates, state_in, fresh,
    out,
    k0, v0, k1, v1, qs, os_, rt, rtp, s0, so, s1, s2, s3,
    kt0, rv0, rvt0, kt1, rv1, rvt1, act, d1, d3, pa,
    gx, gxr, gb, gg, rin, rhalf, rout,
    sqp, sqs, sqz, sqo,
    load_sem, xs, xr, gxs, gxrs, rs_s, rs_r, ag_s, ag_r, ho_s, ho_r, st_s, st_r,
    pp_s, pp_r, zz_s, zz_r, zo_s, zo_r, os_s, os_r,
):
    nz, nh, tok, dh, df, heads_all = sizes
    rows = dh // nz
    half = rows // 2
    nb, ng = df // LANES, df // GROUP
    per = nb // ng
    c, t, h = lax.axis_index("ctx"), lax.axis_index("tok"), lax.axis_index("head")
    z, core = t // 2, t % 2
    other = 1 - core
    np_ = 2 * nh
    me_p = h * 2 + core

    def zdev(step):
        return (c, lax.rem(z + step + nz, nz) * 2 + core, h)

    def pdev(j):
        p = lax.rem(me_p + j, np_)
        return (c, z * 2 + lax.rem(p, 2), p // 2)

    def odev(step):
        return (1 - c, lax.rem(z + step, nz) * 2 + core, h)

    mate = (c, z * 2 + other, h)
    twin = (1 - c, t, h)

    local = [
        (keys.at[0, 0, other], k0.at[1]),
        (state_in.at[0, other], s0.at[1]),
        (values.at[0, 0, other], v0.at[1]),
        (rates, rt),
        (keys.at[0, 0, core], k0.at[0]),
        (state_in.at[0, core], s0.at[0]),
        (values.at[0, 0, core], v0.at[0]),
        (keys.at[1, 0, core], k1.at[0]),
        (values.at[1, 0, core], v1.at[0]),
        (queries.at[0, 0, core], qs.at[0, 0]),
        (queries.at[1, 0, core], qs.at[1, 0]),
    ]
    loads = [pltpu.make_async_copy(a, b, load_sem.at[i]) for i, (a, b) in enumerate(local)]
    for i in (0, 1, 2, 3):
        loads[i].start()
    fresh_load = pltpu.make_async_copy(fresh.at[core], s2, load_sem.at[len(local)])

    barrier = pltpu.get_barrier_semaphore()
    for j in range(1, np_):
        pl.semaphore_signal(barrier, inc=1, device_id=pdev(j), device_id_type=MESH)
    for j in range(1, nz):
        pl.semaphore_signal(barrier, inc=1, device_id=zdev(j), device_id_type=MESH)
    for j in range(nz):
        pl.semaphore_signal(barrier, inc=1, device_id=odev(j), device_id_type=MESH)

    def remote(src, dst, ss, rs, dev):
        return pltpu.make_async_remote_copy(
            src_ref=src, dst_ref=dst, send_sem=ss, recv_sem=rs, device_id=dev, device_id_type=MESH
        )

    def rate_columns(ref, tick, head):
        row = jnp.where(head == 0, ref[tick, 0, 0:1, :], ref[tick, 0, 1:2, :])
        col = jnp.broadcast_to(row, (128, tok)).T
        return jnp.concatenate([col] * (dh // 128), axis=1)

    def prepare(k, v, col, kt, rv, rvt, lo):
        kt[:, lo:lo + tok] = k[...].T
        weighted = (v[...].astype(F32) * col).astype(BF16)
        rv[lo:lo + tok, :] = weighted
        rvt[:, lo:lo + tok] = weighted.T

    def forward(k, rv, state, lo, g):
        at, cols = slice(lo, lo + tok), slice(g * GROUP, (g + 1) * GROUP)
        kk = k[...]
        h1 = jnp.dot(kk, state[0, :, cols], preferred_element_type=F32)
        h3 = jnp.dot(kk, state[1, :, cols], preferred_element_type=F32)
        dact = jnp.dot(rv[at, :], state[2, :, cols], preferred_element_type=F32)
        sig = sigmoid(h1)
        hs = h1 * sig
        act[at, cols] = (hs * h3).astype(BF16)
        d3[at, cols] = (dact * hs).astype(BF16)
        d1[at, cols] = (dact * h3 * (sig + hs * (1.0 - sig))).astype(BF16)

    def grad(m, kt, rvt, lo, hi, g):
        left, right = ((kt, d1), (kt, d3), (rvt, act))[m]
        cols = slice(g * GROUP, (g + 1) * GROUP)
        return jnp.dot(left[:, lo:hi], right[lo:hi, cols], preferred_element_type=F32)

    def blocks(g):
        return range(g * per, (g + 1) * per)

    def lanes(b):
        return slice((b % per) * LANES, (b % per + 1) * LANES)

    order = (2, 0, 1)
    everyb = tuple(range(nb))

    for i in (4, 5, 6):
        loads[i].start()
    for i in (0, 1, 2, 3):
        loads[i].wait()
    prepare(k0.at[1], v0.at[1], rate_columns(rt, 0, other), kt0, rv0, rvt0, 0)
    for i in (7, 8, 9, 10):
        loads[i].start()

    @pl.when(c == 0)
    def _():
        fresh_load.start()

    for g in range(ng):
        forward(k0.at[1], rv0, s0.at[1], 0, g)
        for m in order:
            part = grad(m, kt0, rvt0, 0, tok, g).astype(BF16)
            for b in blocks(g):
                gx[b, m] = part[:, lanes(b)]

    pl.semaphore_wait(barrier, np_ - 1 + nz - 1 + nz)

    gx_copies = [
        remote(gx.at[pl.ds(g * per, per)], gxr.at[pl.ds(g * per, per)], gxs.at[g], gxrs.at[g], mate) for g in range(ng)
    ]
    for cp in gx_copies:
        cp.start()
    state_copies = {m: remote(s0.at[0, m], so.at[m], st_s.at[m], st_r.at[m], twin) for m in order}
    for i in (4, 5, 6):
        loads[i].wait()

    @pl.when(c == 0)
    def _():
        state_copies[order[0]].start()
        state_copies[order[1]].start()

    mate_copies = [
        remote(src, dst, xs.at[i], xr.at[i], mate)
        for i, (src, dst) in enumerate([
            (rates, rtp),
            (keys.at[1, 0, other], k1.at[1]),
            (values.at[1, 0, other], v1.at[1]),
            (queries.at[0, 0, other], qs.at[0, 1]),
            (queries.at[1, 0, other], qs.at[1, 1]),
        ])
    ]

    def chunk(owner_step, part=None):
        owner = lax.rem(z + owner_step + 2 * nz, nz)
        if part is None:
            return (slice(None), pl.ds(pl.multiple_of(owner * rows, rows), rows), slice(None))
        return (slice(None), pl.ds(pl.multiple_of(owner * rows + part * half, half), half), slice(None))

    sides = ((0, -1), (1, 1))

    def rs_copy(tick, hop, d, s, b):
        if hop == 0:
            src, dst, dev = gb.at[(tick, b) + chunk(3 * s)], rin.at[tick, 0, d, b], zdev(s)
        elif hop == 1:
            src, dst, dev = gb.at[(tick, b) + chunk(4, d)], rhalf.at[tick, d, b], zdev(3 * s)
        else:
            src, dst, dev = rout.at[tick, hop - 2, d, b], rin.at[tick, hop - 1, d, b], zdev(s)
        return remote(src, dst, rs_s.at[tick, hop, d, b], rs_r.at[tick, hop, d, b], dev)

    def rs_first(tick, b):
        for d, s in sides:
            rs_copy(tick, 0, d, s, b).start()

    def rs_far(tick, b):
        for d, s in sides:
            rs_copy(tick, 1, d, s, b).start()

    def rs_second(tick, b):
        for d, s in sides:
            rs_copy(tick, 0, d, s, b).wait_recv()
            own = gb[(tick, b) + chunk(2 * s)].astype(F32) + rin[tick, 0, d, b].astype(F32)
            rout[tick, 0, d, b] = own.astype(BF16)
            rs_copy(tick, 2, d, s, b).start()

    def rs_third(tick, b):
        for d, s in sides:
            rs_copy(tick, 2, d, s, b).wait_recv()
            rs_copy(tick, 1, d, s, b).wait_recv()
            own = gb[(tick, b) + chunk(s)].astype(F32) + rin[tick, 1, d, b].astype(F32)
            far = rhalf[tick, d, b].astype(F32)
            if d == 0:
                rout[tick, 1, d, b, :, 0:half, :] = (own[:, 0:half] + far).astype(BF16)
                rout[tick, 1, d, b, :, half:rows, :] = own[:, half:rows].astype(BF16)
            else:
                rout[tick, 1, d, b, :, 0:half, :] = own[:, 0:half].astype(BF16)
                rout[tick, 1, d, b, :, half:rows, :] = (own[:, half:rows] + far).astype(BF16)
            rs_copy(tick, 3, d, s, b).start()

    def rs_last(tick, b, buf):
        total = gb[(tick, b) + chunk(0)].astype(F32)
        for d, s in sides:
            rs_copy(tick, 3, d, s, b).wait_recv()
            total = total + rin[tick, 2, d, b].astype(F32)
        gg[(buf, b) + chunk(0)] = total.astype(BF16)
        square = total * total
        tile = jnp.zeros((8, 128), F32)
        for m in range(3):
            for i in range(0, rows, 8):
                tile = tile + square[m, i:i + 8]
        return tile

    def ag_copy(buf, hop, d, s, b):
        if hop == 0:
            part, dev = chunk(0), zdev(s)
        elif hop == 1:
            part, dev = chunk(-s), zdev(s)
        elif hop == 2:
            part, dev = chunk(-2 * s), zdev(s)
        elif buf == 0:
            part, dev = chunk(-3 * s, d), zdev(s)
        else:
            part, dev = chunk(-s, d), zdev(3 * s)
        part = (buf, b) + part
        return remote(gg.at[part], gg.at[part], ag_s.at[buf, hop, d, b], ag_r.at[buf, hop, d, b], dev)

    def ag_first(buf, b):
        for d, s in sides:
            ag_copy(buf, 0, d, s, b).start()

    def ag_second(buf):
        for b in everyb:
            for d, s in sides:
                ag_copy(buf, 0, d, s, b).wait_recv()
                ag_copy(buf, 1, d, s, b).start()
        if buf != 0:
            for b in everyb:
                for d, s in sides:
                    ag_copy(buf, 3, d, s, b).start()

    def ag_third(buf):
        for b in everyb:
            for d, s in sides:
                ag_copy(buf, 1, d, s, b).wait_recv()
                ag_copy(buf, 2, d, s, b).start()

    def ag_fourth(buf):
        for b in everyb:
            for d, s in sides:
                ag_copy(buf, 2, d, s, b).wait_recv()
                ag_copy(buf, 3, d, s, b).start()

    def ag_last(buf, b):
        for d, s in sides:
            ag_copy(buf, 3, d, s, b).wait_recv()
            if buf != 0:
                ag_copy(buf, 2, d, s, b).wait_recv()

    def plane_copy(tick, j):
        return remote(sqp.at[tick, me_p], sqp.at[tick, me_p], pp_s.at[tick, j], pp_r.at[tick, j], pdev(j))

    def norm_first(tick, tile):
        sqp[tick, me_p] = tile
        for j in range(1, np_):
            plane_copy(tick, j).start()

    def z_copy(tick, j):
        return remote(sqs.at[tick], sqz.at[tick, z], zz_s.at[tick, j], zz_r.at[tick, j], zdev(j))

    def zo_copy(j):
        return remote(sqs.at[0], sqo.at[z], zo_s.at[j], zo_r.at[j], odev(j))

    def norm_second(tick):
        for j in range(1, np_):
            plane_copy(tick, j).wait_recv()
        total = sqp[tick, 0]
        for j in range(1, np_):
            total = total + sqp[tick, j]
        sqs[tick] = total
        sqz[tick, z] = total
        for j in range(1, nz):
            z_copy(tick, j).start()
        if tick == 0:
            @pl.when(c == 0)
            def _():
                for j in range(nz):
                    zo_copy(j).start()

    def scale_of(ref):
        total = ref[0]
        for j in range(1, nz):
            total = total + ref[j]
        sq = jnp.sum(jnp.sum(total, axis=1, keepdims=True), axis=0, keepdims=True)
        return 0.5 * jnp.sqrt(jnp.float32(3 * df * heads_all)) / jnp.sqrt(sq + 1e-06)

    def renorm(old, buf, scale, new, b):
        cols = slice(b * LANES, (b + 1) * LANES)
        for m in range(3):
            older = old[m, :, cols].astype(F32)
            moved = older + scale * gg[buf, b, m].astype(F32)
            was = jnp.sum(older * older, axis=0, keepdims=True)
            now = jnp.sum(moved * moved, axis=0, keepdims=True)
            factor = jnp.sqrt(was) / jnp.sqrt(now + 1e-06)
            new[m, :, cols] = (moved * factor).astype(BF16)

    def mix(tick, part, state, g):
        cols = slice(g * GROUP, (g + 1) * GROUP)
        q = qs[tick, part]
        p1 = jnp.dot(q, state[0, :, cols], preferred_element_type=F32)
        p3 = jnp.dot(q, state[1, :, cols], preferred_element_type=F32)
        pa[part, :, cols] = (p1 * sigmoid(p1) * p3).astype(BF16)

    tiles = tok // GROUP

    def mate_out(tick, i):
        at = pl.ds(i * GROUP, GROUP)
        return remote(os_.at[tick, at], out.at[tick, 0, core, at], os_s.at[tick, i], os_r.at[tick, i], mate)

    def apply_mate(tick, state):
        for i in range(tiles):
            at = slice(i * GROUP, (i + 1) * GROUP)
            o = lax.dot_general(pa[1, at], state[2], NT, preferred_element_type=F32)
            os_[tick, at, :] = o.astype(BF16)
            mate_out(tick, i).start()

    def apply_own(tick, state):
        o = lax.dot_general(pa[0], state[2], NT, preferred_element_type=F32)
        out[tick, 0, core] = o.astype(BF16)

    prepare(k0.at[0], v0.at[0], rate_columns(rt, 0, core), kt0, rv0, rvt0, tok)
    for g in range(ng):
        forward(k0.at[0], rv0, s0.at[0], tok, g)
        for m in order:
            part = grad(m, kt0, rvt0, tok, 2 * tok, g).astype(BF16).astype(F32)
            if m == order[0]:
                gx_copies[g].wait_recv()
            for b in blocks(g):
                gb[0, b, m] = (part[:, lanes(b)] + gxr[b, m].astype(F32)).astype(BF16)
        for b in blocks(g):
            rs_first(0, b)
        for b in blocks(g):
            rs_far(0, b)
    for cp in mate_copies:
        cp.start()
    loads[7].wait()
    loads[8].wait()
    prepare(k1.at[0], v1.at[0], rate_columns(rt, 1, core), kt1, rv1, rvt1, 0)
    for b in everyb:
        rs_second(0, b)
    for i in (0, 1, 2):
        mate_copies[i].wait_recv()
    prepare(k1.at[1], v1.at[1], rate_columns(rtp, 1, core), kt1, rv1, rvt1, tok)
    for b in everyb:
        rs_third(0, b)

    def hand_over(b):
        part = (b,) + chunk(0)
        return remote(gg.at[(0,) + part], gg.at[(1,) + part], ho_s.at[b], ho_r.at[b], twin)

    tile = jnp.zeros((8, 128), F32)
    for b in everyb:
        tile = tile + rs_last(0, b, 0)

        @pl.when(c == 0)
        def _():
            hand_over(b).start()

        ag_first(0, b)
    norm_first(0, tile)

    @pl.when(c == 0)
    def _():
        state_copies[order[2]].start()
        ag_second(0)

    @pl.when(c == 1)
    def _():
        for b in everyb:
            hand_over(b).wait_recv()
            ag_first(1, b)

    norm_second(0)

    @pl.when(c == 1)
    def _():
        ag_second(1)
        ag_third(1)
        for j in range(nz):
            zo_copy(j).wait_recv()
        for m in order:
            state_copies[m].wait_recv()

    @pl.when(c == 0)
    def _():
        fresh_load.wait()

    for g in range(ng):
        @pl.when(c == 1)
        def _():
            for b in blocks(g):
                ag_last(1, b)
            if g == 0:
                ag_second(0)
            scale = scale_of(sqo)
            for b in blocks(g):
                renorm(so, 1, scale, s2, b)

        forward(k1.at[0], rv1, s2, 0, g)
        forward(k1.at[1], rv1, s2, tok, g)
        for m in order:
            part = grad(m, kt1, rvt1, 0, 2 * tok, g).astype(BF16)
            for b in blocks(g):
                gb[1, b, m] = part[:, lanes(b)]
        for b in blocks(g):
            rs_first(1, b)
        for b in blocks(g):
            rs_far(1, b)
    for b in everyb:
        rs_second(1, b)
    for b in everyb:
        rs_third(1, b)
    ag_third(0)
    tile = jnp.zeros((8, 128), F32)
    for b in everyb:
        tile = tile + rs_last(1, b, 2)
        ag_first(2, b)
    norm_first(1, tile)
    ag_second(2)
    norm_second(1)
    ag_fourth(0)
    ag_third(2)
    for j in range(1, nz):
        z_copy(0, j).wait_recv()
    loads[9].wait()
    mate_copies[3].wait_recv()
    scale = scale_of(sqz.at[0])
    for b in everyb:
        ag_last(0, b)
        renorm(s0.at[0], 0, scale, s1, b)
    for g in range(ng):
        for part in (0, 1):
            mix(0, part, s1, g)
    apply_mate(0, s1)
    apply_own(0, s1)
    loads[10].wait()
    mate_copies[4].wait_recv()
    for j in range(1, nz):
        z_copy(1, j).wait_recv()
    scale = scale_of(sqz.at[1])
    for g in range(ng):
        for b in blocks(g):
            ag_last(2, b)
            renorm(s2, 2, scale, s3, b)
        for part in (1, 0):
            mix(1, part, s3, g)
    apply_mate(1, s3)
    apply_own(1, s3)

    for cp in gx_copies + mate_copies:
        cp.wait_send()
    for b in everyb:
        for tick in (0, 1):
            for hop in range(4):
                for d, s in sides:
                    rs_copy(tick, hop, d, s, b).wait_send()
        for buf in (0, 2):
            for hop in range(4):
                for d, s in sides:
                    ag_copy(buf, hop, d, s, b).wait_send()
    for tick in (0, 1):
        for j in range(1, np_):
            plane_copy(tick, j).wait_send()
        for j in range(1, nz):
            z_copy(tick, j).wait_send()

    @pl.when(c == 0)
    def _():
        for m in order:
            state_copies[m].wait_send()
        for b in everyb:
            hand_over(b).wait_send()
        for j in range(nz):
            zo_copy(j).wait_send()

    @pl.when(c == 1)
    def _():
        for b in everyb:
            for hop in range(4):
                for d, s in sides:
                    ag_copy(1, hop, d, s, b).wait_send()

    for tick in (0, 1):
        for i in range(tiles):
            mate_out(tick, i).wait()


def shards(mesh_shape, keys, values, queries, rates, state_in, fresh):
    nz, nh = mesh_shape["tok"] // 2, mesh_shape["head"]
    _, _, _, tok, dh = keys.shape
    df = state_in.shape[-1]
    heads_all = 2 * nh
    rows, nb = dh // nz, df // LANES
    cut = (nb, 3, dh, LANES)
    sizes = (nz, nh, tok, dh, df, heads_all)
    dma = pltpu.SemaphoreType.DMA

    def vm(*shape, dtype=BF16):
        return pltpu.VMEM(shape, dtype)

    both = 2 * tok
    state = (3, dh, df)
    scratch = [
        vm(2, tok, dh), vm(2, tok, dh), vm(2, tok, dh), vm(2, tok, dh), vm(2, 2, tok, dh), vm(2, tok, dh),
        vm(*rates.shape, dtype=F32), vm(*rates.shape, dtype=F32),
        vm(2, *state), vm(*state), vm(*state), vm(*state), vm(*state),
        vm(dh, both), vm(both, dh), vm(dh, both), vm(dh, both), vm(both, dh), vm(dh, both),
        vm(both, df), vm(both, df), vm(both, df), vm(2, tok, df),
        vm(*cut), vm(*cut), vm(2, *cut), vm(3, *cut),
        vm(2, 3, 2, nb, 3, rows, LANES), vm(2, 2, nb, 3, rows // 2, LANES), vm(2, 2, 2, nb, 3, rows, LANES),
        vm(2, 2 * nh, 8, 128, dtype=F32), vm(2, 8, 128, dtype=F32), vm(2, nz, 8, 128, dtype=F32), vm(nz, 8, 128, dtype=F32),
        dma((12,)), dma((5,)), dma((5,)), dma((3,)), dma((3,)),
        dma((2, 4, 2, nb)), dma((2, 4, 2, nb)), dma((3, 4, 2, nb)), dma((3, 4, 2, nb)),
        dma((nb,)), dma((nb,)), dma((3,)), dma((3,)),
        dma((2, 2 * nh)), dma((2, 2 * nh)), dma((2, nz)), dma((2, nz)), dma((nz,)), dma((nz,)),
        dma((2, tok // GROUP)), dma((2, tok // GROUP)),
    ]
    return pl.pallas_call(
        functools.partial(kernel, sizes),
        out_shape=pltpu.VMEM(queries.shape, BF16),
        in_specs=[pl.BlockSpec(memory_space=pltpu.HBM)] * 6,
        out_specs=pl.BlockSpec(memory_space=pltpu.VMEM),
        scratch_shapes=scratch,
        compiler_params=pltpu.CompilerParams(
            collective_id=0, has_side_effects=True, vmem_limit_bytes=40 * 1024 * 1024
        ),
        cost_estimate=pl.CostEstimate(flops=8_000_000_000, bytes_accessed=10_000_000, transcendentals=3_000_000),
    )(*(pltpu.with_memory_space_constraint(a, pltpu.HBM) for a in (keys, values, queries, rates, state_in, fresh)))


def solution(mesh):
    in_specs = (
        P(None, "ctx", "head", "tok", None),
        P(None, "ctx", "head", "tok", None),
        P(None, "ctx", "head", "tok", None),
        P(None, "ctx", "head", "tok"),
        P("ctx", "head", None, None, None),
        P("head", None, None, None),
    )
    return jax.shard_map(
        functools.partial(shards, dict(mesh.shape)),
        mesh=mesh,
        in_specs=in_specs,
        out_specs=P(None, "ctx", "head", "tok", None),
        check_vma=False,
    )
```

time: 82 us -> 78.3 us (0.955)
  Pallas kernels: 79.3 us -> 77 us
  local copies, waits for them, and re-layouts: 2.65 us -> 1.15 us
    pallas_call x1, Pallas kernels: 79.3 us -> 77 us  [shards(): pl.pallas_call(functools.partial(kernel, sizes), out_shape=pltpu.VMEM(que...]
    unnamed x1, local copies, waits for them, and re-layouts: 2.65 us -> 1.15 us
where the time goes in v2:
time: 78.3 us; the launch traced here: 78.1 us
  Pallas kernels  77 us (98%)
  local copies, waits for them, and re-layouts  1.15 us (1%)
    pallas_call x1, Pallas kernels, shards(): pl.pallas_call(functools.partial(kernel, sizes), out_shape=pltpu.VMEM(que...  77 us

profile of v2, /device:TPU:5, one launch (start us, length us, event | category | flops | bytes accessed | tf_op | source)
XLA Modules:
  0.0 78.1 jit_solution(8665882114253355866)
XLA Ops:
  0.0 77.0 %shard_map.64 = bf16[2,1,2,768,256]{4,3,2,1,0:T(8,128)(2,1)S(1)} custom-call(bf16[2,1,2,768,256]{4,3,2,1,0:T(8,128)(2,1)} %keys.1, bf16[2,1,2,768,256]{4,3,2,1,0:T(8,128)(2,1)} %values.1, bf16[2,1,2,768,256]{4,3,2,1,0:T(8,128)(2,1)} %queries.1, f32[2,1,2,768]{3,2,1,0:T(2,128)} %rates.1, bf16[1,2,3,256,512]{4,3,2,1,0:T(8,128)(2,1)} %state_in.1, ...), custom_call_target="tpu_custom_call" | custom-call | flops 8000000000 | bytes 10000000 | tf_op jit(solution)/shard_map/pallas_call | solution.py:542
  77.0 1.1 %copy.8 = bf16[2,1,2,768,256]{4,3,2,1,0:T(8,128)(2,1)} copy(bf16[2,1,2,768,256]{4,3,2,1,0:T(8,128)(2,1)S(1)} %shard_map.64) | data formatting | bytes 3145728

commit v3 on v2

--- a/solution.py
+++ b/solution.py
@@ -432,18 +432,15 @@
             rs_far(1, b)
     for b in everyb:
         rs_second(1, b)
+    ag_third(0)
     for b in everyb:
         rs_third(1, b)
-    ag_third(0)
+    ag_fourth(0)
     tile = jnp.zeros((8, 128), F32)
     for b in everyb:
         tile = tile + rs_last(1, b, 2)
         ag_first(2, b)
     norm_first(1, tile)
-    ag_second(2)
-    norm_second(1)
-    ag_fourth(0)
-    ag_third(2)
     for j in range(1, nz):
         z_copy(0, j).wait_recv()
     loads[9].wait()
@@ -452,10 +449,15 @@
     for b in everyb:
         ag_last(0, b)
         renorm(s0.at[0], 0, scale, s1, b)
-    for g in range(ng):
+    for part in (0, 1):
+        mix(0, part, s1, 0)
+    ag_second(2)
+    norm_second(1)
+    for g in range(1, ng):
         for part in (0, 1):
             mix(0, part, s1, g)
     apply_mate(0, s1)
+    ag_third(2)
     apply_own(0, s1)
     loads[10].wait()
     mate_copies[4].wait_recv()

time: 78.3 us -> 76.2 us (0.973)
  Pallas kernels: 77 us -> 75 us
    pallas_call x1, Pallas kernels: 77 us -> 75 us  [shards(): pl.pallas_call(functools.partial(kernel, sizes), out_shape=pltpu.VMEM(que...]
where the time goes in v3:
time: 76.2 us; the launch traced here: 76.1 us
  Pallas kernels  75 us (98%)
  local copies, waits for them, and re-layouts  1.15 us (2%)
    pallas_call x1, Pallas kernels, shards(): pl.pallas_call(functools.partial(kernel, sizes), out_shape=pltpu.VMEM(que...  75 us

profile of v3, /device:TPU:5, one launch (start us, length us, event | category | flops | bytes accessed | tf_op | source)
XLA Modules:
  0.0 76.1 jit_solution(17101093324410078152)
XLA Ops:
  0.0 75.0 %shard_map.64 = bf16[2,1,2,768,256]{4,3,2,1,0:T(8,128)(2,1)S(1)} custom-call(bf16[2,1,2,768,256]{4,3,2,1,0:T(8,128)(2,1)} %keys.1, bf16[2,1,2,768,256]{4,3,2,1,0:T(8,128)(2,1)} %values.1, bf16[2,1,2,768,256]{4,3,2,1,0:T(8,128)(2,1)} %queries.1, f32[2,1,2,768]{3,2,1,0:T(2,128)} %rates.1, bf16[1,2,3,256,512]{4,3,2,1,0:T(8,128)(2,1)} %state_in.1, ...), custom_call_target="tpu_custom_call" | custom-call | flops 8000000000 | bytes 10000000 | tf_op jit(solution)/shard_map/pallas_call | solution.py:544
  75.0 1.1 %copy.8 = bf16[2,1,2,768,256]{4,3,2,1,0:T(8,128)(2,1)} copy(bf16[2,1,2,768,256]{4,3,2,1,0:T(8,128)(2,1)S(1)} %shard_map.64) | data formatting | bytes 3145728

commit v4 on v3

--- a/solution.py
+++ b/solution.py
@@ -244,14 +244,15 @@
             ag_copy(buf, 0, d, s, b).start()
 
     def ag_second(buf):
-        for b in everyb:
-            for d, s in sides:
-                ag_copy(buf, 0, d, s, b).wait_recv()
-                ag_copy(buf, 1, d, s, b).start()
-        if buf != 0:
-            for b in everyb:
+        for g in range(ng):
+            for b in blocks(g):
                 for d, s in sides:
-                    ag_copy(buf, 3, d, s, b).start()
+                    ag_copy(buf, 0, d, s, b).wait_recv()
+                    ag_copy(buf, 1, d, s, b).start()
+            if buf != 0:
+                for b in blocks(g):
+                    for d, s in sides:
+                        ag_copy(buf, 3, d, s, b).start()
 
     def ag_third(buf):
         for b in everyb:

time: 76.2 us -> 76 us (level)
  no operation moved by 1% of the time
where the time goes in v4:
time: 76 us; the launch traced here: 75.9 us
  Pallas kernels  74.7 us (98%)
  local copies, waits for them, and re-layouts  1.15 us (2%)
    pallas_call x1, Pallas kernels, shards(): pl.pallas_call(functools.partial(kernel, sizes), out_shape=pltpu.VMEM(que...  74.7 us

profile of v4, /device:TPU:5, one launch (start us, length us, event | category | flops | bytes accessed | tf_op | source)
XLA Modules:
  0.0 75.9 jit_solution(8545557963873012106)
XLA Ops:
  0.0 74.7 %shard_map.64 = bf16[2,1,2,768,256]{4,3,2,1,0:T(8,128)(2,1)S(1)} custom-call(bf16[2,1,2,768,256]{4,3,2,1,0:T(8,128)(2,1)} %keys.1, bf16[2,1,2,768,256]{4,3,2,1,0:T(8,128)(2,1)} %values.1, bf16[2,1,2,768,256]{4,3,2,1,0:T(8,128)(2,1)} %queries.1, f32[2,1,2,768]{3,2,1,0:T(2,128)} %rates.1, bf16[1,2,3,256,512]{4,3,2,1,0:T(8,128)(2,1)} %state_in.1, ...), custom_call_target="tpu_custom_call" | custom-call | flops 8000000000 | bytes 10000000 | tf_op jit(solution)/shard_map/pallas_call | solution.py:545
  74.8 1.1 %copy.8 = bf16[2,1,2,768,256]{4,3,2,1,0:T(8,128)(2,1)} copy(bf16[2,1,2,768,256]{4,3,2,1,0:T(8,128)(2,1)S(1)} %shard_map.64) | data formatting | bytes 3145728

commit v5 on v4

--- a/solution.py
+++ b/solution.py
@@ -277,7 +277,7 @@
 
     def norm_first(tick, tile):
         sqp[tick, me_p] = tile
-        for j in range(1, np_):
+        for j in sorted(range(1, np_), key=lambda j: abs(j - nh)):
             plane_copy(tick, j).start()
 
     def z_copy(tick, j):
@@ -294,13 +294,13 @@
             total = total + sqp[tick, j]
         sqs[tick] = total
         sqz[tick, z] = total
-        for j in range(1, nz):
-            z_copy(tick, j).start()
         if tick == 0:
             @pl.when(c == 0)
             def _():
-                for j in range(nz):
+                for j in sorted(range(nz), key=lambda j: abs(j - nz // 2)):
                     zo_copy(j).start()
+        for j in sorted(range(1, nz), key=lambda j: abs(j - nz // 2)):
+            z_copy(tick, j).start()
 
     def scale_of(ref):
         total = ref[0]
@@ -387,7 +387,6 @@
     @pl.when(c == 0)
     def _():
         state_copies[order[2]].start()
-        ag_second(0)
 
     @pl.when(c == 1)
     def _():
@@ -396,6 +395,10 @@
             ag_first(1, b)
 
     norm_second(0)
+
+    @pl.when(c == 0)
+    def _():
+        ag_second(0)
 
     @pl.when(c == 1)
     def _():

time: 76 us -> 76 us (level)
  no operation moved by 1% of the time
where the time goes in v5:
time: 76 us; the launch traced here: 75.9 us
  Pallas kernels  74.8 us (98%)
  local copies, waits for them, and re-layouts  1.15 us (2%)
    pallas_call x1, Pallas kernels, shards(): pl.pallas_call(functools.partial(kernel, sizes), out_shape=pltpu.VMEM(que...  74.8 us

profile of v5, /device:TPU:5, one launch (start us, length us, event | category | flops | bytes accessed | tf_op | source)
XLA Modules:
  0.0 75.9 jit_solution(10955990165759857620)
XLA Ops:
  0.0 74.8 %shard_map.64 = bf16[2,1,2,768,256]{4,3,2,1,0:T(8,128)(2,1)S(1)} custom-call(bf16[2,1,2,768,256]{4,3,2,1,0:T(8,128)(2,1)} %keys.1, bf16[2,1,2,768,256]{4,3,2,1,0:T(8,128)(2,1)} %values.1, bf16[2,1,2,768,256]{4,3,2,1,0:T(8,128)(2,1)} %queries.1, f32[2,1,2,768]{3,2,1,0:T(2,128)} %rates.1, bf16[1,2,3,256,512]{4,3,2,1,0:T(8,128)(2,1)} %state_in.1, ...), custom_call_target="tpu_custom_call" | custom-call | flops 8000000000 | bytes 10000000 | tf_op jit(solution)/shard_map/pallas_call | solution.py:548
  74.8 1.1 %copy.8 = bf16[2,1,2,768,256]{4,3,2,1,0:T(8,128)(2,1)} copy(bf16[2,1,2,768,256]{4,3,2,1,0:T(8,128)(2,1)S(1)} %shard_map.64) | data formatting | bytes 3145728
